TPU v7x, 512 devices: a whole 4x4x16 slice. The times are simulated.
512 devices in a mesh: row: 32 (over x, z_lo), col: 16 (over y, z_hi, core).
Axes of the slice: x: 4, y: 4, z: 16 (z_hi: 2, z_lo: 8; z = z_hi * 8 + z_lo), core: 2. Of those that a mesh axis runs over, the one named last changes fastest.
Arguments:
- density: bfloat16 [256, 16, 2, 128, 128], P('row', 'col'), may hold values from -0.26953125 to 0.26953125
- pattern: int32 [256, 16, 2], P('row', 'col'), may hold values from 0 to 15, as said below
- kept_pattern: int32 [256, 16, 4], P('row', 'col'), may hold values from 0 to 15, as said below
Outputs:
- purified: bfloat16 [256, 16, 4, 128, 128], P('row', 'col')
Inputs may be any that keep to these rules, and one draw needn't show every extreme that they name: `pattern`: in each block row and tile the 2 entries are distinct block columns of that tile, numbered within it. `kept_pattern`: in each block row and tile the 4 entries are distinct block columns of that tile, numbered within it.
All inputs are finite; a program needn't handle non-finite values.
Results may differ from a plain program's by a relative error of at most 0.005.
Values may be sent and summed in bfloat16 or wider, within the bound.
A program may use at most 64 MiB of HBM per device.

v0:
```python
import jax
import jax.numpy as jnp
from jax import lax
from jax.sharding import PartitionSpec as P

ST = 4


def shifted(block, axis, distance):
    devices = range(lax.axis_size(axis))
    route = [(i - distance, i) for i in devices if i - distance in devices]
    return lax.ppermute(block, axis, route)


def broadcast(array, axis, root):
    mine = lax.axis_index(axis) == root
    return lax.psum(jnp.where(mine, array, jnp.zeros_like(array)), axis)


def shortened(array):

    def short(part):
        return part.astype(jnp.bfloat16) if part.dtype == jnp.float32 else part

    return jax.tree.map(short, array)


def shifted_2(value, axis, steps):
    count = lax.axis_size(axis)
    pairs = [(source, (source + steps) % count) for source in range(count)]
    return lax.ppermute(value, axis, pairs)


def section_terms(left_blocks, left_index, right_blocks, right_index, kept_index):
    picked = jnp.take(right_blocks, left_index, axis=0)
    picked_index = jnp.take(right_index, left_index, axis=0)
    products = jnp.einsum(
        "aixy,aijyz->aijxz", left_blocks, picked, preferred_element_type=jnp.float32
    )
    matches = (picked_index[..., None] == kept_index[:, None, None, :]).astype(jnp.float32)
    return jnp.einsum("aijt,aijxz->atxz", matches, products, precision=lax.Precision.HIGHEST)


def windowed_product(left_pair, right_sections, kept_index, advance):
    left_blocks, left_index = left_pair
    summed = jnp.zeros(
        (left_blocks.shape[0], kept_index.shape[1]) + left_blocks.shape[2:], jnp.float32
    )
    for section_num in range(len(right_sections)):
        if section_num > 0:
            left_blocks, left_index = advance((left_blocks, left_index))
        summed = summed + section_terms(
            left_blocks,
            left_index,
            right_sections[section_num][0],
            right_sections[section_num][1],
            kept_index,
        )
    return summed


def stack_preceding(own_blocks, own_index):
    block_pieces = []
    index_pieces = []
    moved_blocks, moved_index = shifted((own_blocks, own_index), "row", 1)
    block_pieces.append(moved_blocks)
    index_pieces.append(moved_index)
    block_pieces.append(own_blocks)
    index_pieces.append(own_index)
    return (jnp.concatenate(block_pieces, axis=0), jnp.concatenate(index_pieces, axis=0))


def on_device(density, pattern, kept_pattern):
    own_blocks = density[:, 0]
    own_index = pattern[:, 0]
    kept_index = kept_pattern[:, 0]
    row_count = lax.axis_size("row")
    col_count = lax.axis_size("col")
    ratio = row_count // col_count
    col_place = lax.axis_index("col")
    stacked = stack_preceding(own_blocks, own_index)
    right_sections = [
        (
            broadcast(
                stacked[0], "row", ratio * ((col_place + section_num) % col_count) + ratio - 1
            ),
            broadcast(
                shortened(stacked[1]),
                "row",
                ratio * ((col_place + section_num) % col_count) + ratio - 1,
            ),
        )
        for section_num in range(ST)
    ]
    first = windowed_product(
        (own_blocks, own_index),
        right_sections,
        kept_index,
        lambda pair: jax.tree.map(
            lambda part, own: part.astype(own.dtype),
            shifted_2(shortened(pair), "col", col_count - 1),
            pair,
        ),
    )
    squared = first.astype(jnp.bfloat16)
    cubed = windowed_product(
        (squared, kept_index),
        right_sections,
        kept_index,
        lambda pair: jax.tree.map(
            lambda part, own: part.astype(own.dtype),
            shifted_2(shortened(pair), "col", col_count - 1),
            pair,
        ),
    )
    purified = (3.0 * squared.astype(jnp.float32) - 2.0 * cubed).astype(jnp.bfloat16)
    return purified[:, None]


def solution(mesh):
    in_specs = (P("row", "col", None, None, None), P("row", "col", None), P("row", "col", None))
    out_specs = P("row", "col", None, None, None)
    return jax.shard_map(
        on_device, mesh=mesh, in_specs=in_specs, out_specs=out_specs, check_vma=False
    )
```

profile of v0, /device:TPU:1, one launch (start us, length us, event | category | flops | bytes accessed | tf_op | source)
XLA Modules:
  0.0 791.9 jit_solution(3040481527065091865)
XLA Ops:
  6.5 4.4 collective-permute-start.1
  10.9 5.7 collective-permute-start.3
  16.7 13.6 %collective-permute-start.2 = (s32[8,2]{0,1:T(2,128)}, s32[8,2]{0,1:T(2,128)S(1)}, u32[]{:S(2)}, u32[]{:S(2)}) collective-permute-start(s32[8,2]{0,1:T(2,128)} %bitcast.185), channel_id=1, source_target_pairs={{0,15},{1,0},{2,1},{3,2},{4,3},{5,4},{6,5},{7,6},{8,7},{9,8},{10,9... | collective-permute-start | bytes 200 | tf_op jit(solution)/shard_map/ppermute | solution.py:31
  44.2 13.2 %collective-permute-done.2 = s32[8,2]{0,1:T(2,128)S(1)} collective-permute-done((s32[8,2]{0,1:T(2,128)}, s32[8,2]{0,1:T(2,128)S(1)}, u32[]{:S(2)}, u32[]{:S(2)}) %collective-permute-start.2) | collective-permute-done | bytes 96 | tf_op jit(solution)/shard_map/ppermute | solution.py:31
  57.7 205.8 %all-reduce = (s32[16,2]{1,0:T(8,128)S(1)}, s32[16,2]{1,0:T(8,128)S(1)}, s32[16,2]{1,0:T(8,128)S(1)}, s32[16,2]{1,0:T(8,128)S(1)}) all-reduce(s32[16,2]{1,0:T(8,128)S(1)} %get-tuple-element.22, s32[16,2]{1,0:T(8,128)S(1)} %get-tuple-element.23, s32[16,2]{1,0:T(8,128)S(1)} %get-tuple-element.24, ...), channel_id=1, replica_groups=mesh['row'=32,'col'=16] {'row'}, use_global_device_ids=true, to_apply=%region_4.7 | all-reduce | flops 128 | bytes 1024 | tf_op jit(solution)/shard_map/psum | solution.py:17
  265.9 25.1 %collective-permute-start.4 = (s32[8,2]{0,1:T(2,128)S(1)}, s32[8,2]{0,1:T(2,128)S(1)}, u32[]{:S(2)}, u32[]{:S(2)}) collective-permute-start(s32[8,2]{0,1:T(2,128)S(1)} %collective-permute-done.2), channel_id=1, source_target_pairs={{0,15},{1,0},{2,1},{3,2},{4,3},{5,4},{6,5},{7,6},{8,7},{9,8},{10,9... | collective-permute-start | bytes 200 | tf_op jit(solution)/shard_map/ppermute | solution.py:31
  291.1 5.2 collective-permute-done.4
  300.4 10.4 %collective-permute-start.10 = (s32[8,4]{0,1:T(4,128)S(1)}, s32[8,4]{0,1:T(4,128)S(1)}, u32[]{:S(2)}, u32[]{:S(2)}) collective-permute-start(s32[8,4]{0,1:T(4,128)S(1)} %collective-permute-done.8), channel_id=1, source_target_pairs={{0,15},{1,0},{2,1},{3,2},{4,3},{5,4},{6,5},{7,6},{8,7},{9,8},{10,9... | collective-permute-start | bytes 392 | tf_op jit(solution)/shard_map/ppermute | solution.py:31
  316.5 33.0 %collective-permute-done.5 = bf16[8,2,128,128]{3,2,1,0:T(8,128)(2,1)} collective-permute-done((bf16[8,2,128,128]{3,2,1,0:T(8,128)(2,1)S(1)}, bf16[8,2,128,128]{3,2,1,0:T(8,128)(2,1)}, u32[]{:S(2)}, u32[]{:S(2)}) %collective-permute-start.5) | collective-permute-done | bytes 524320 | tf_op jit(solution)/shard_map/ppermute | solution.py:31
  351.9 195.2 %all-reduce.4.cloned.1.call-done = (bf16[16,2,128,128]{3,2,1,0:T(8,128)(2,1)}, bf16[16,2,128,128]{3,2,1,0:T(8,128)(2,1)}, bf16[16,2,128,128]{3,2,1,0:T(8,128)(2,1)}, bf16[16,2,128,128]{3,2,1,0:T(8,128)(2,1)}) async-done(((bf16[16,2,128,128]{3,2,1,0:T(8,128)(2,1)}, bf16[16,2,128,128]{3,2,1,0:T(8,128)(2,1)}, bf16[16,2,128,128]{3,2,1,0:T(8,128)(2,1)}, bf16[16,2,128,128]{3,2,1,0:T(8,128)(2,1)}), ...) | async-done | bytes 4194320 | tf_op jit(solution)/shard_map/psum | solution.py:17
  558.0 4.2 copy.128
  567.5 4.2 copy.119
  578.9 4.2 copy.146
  583.1 5.1 fusion.45
  595.9 5.5 fusion.3
  601.4 22.7 %collective-permute-start.9 = (bf16[8,4,128,128]{3,1,2,0:T(4,128)(2,1)}, bf16[8,4,128,128]{3,1,2,0:T(4,128)(2,1)}, u32[]{:S(2)}, u32[]{:S(2)}) collective-permute-start(bf16[8,4,128,128]{3,1,2,0:T(4,128)(2,1)} %fusion.3), channel_id=1, source_target_pairs={{0,15},{1,0},{2,1},{3,2},{4,3},{5,4},{6,5},{7,6},{8,7},{9,8},{10,9... | collective-permute-start | bytes 3145736 | tf_op jit(solution)/shard_map/ppermute | solution.py:31
  627.0 33.3 %collective-permute-done.12 = s32[8,4]{0,1:T(4,128)S(1)} collective-permute-done((s32[8,4]{0,1:T(4,128)S(1)}, s32[8,4]{0,1:T(4,128)S(1)}, u32[]{:S(2)}, u32[]{:S(2)}) %collective-permute-start.12) | collective-permute-done | bytes 160 | tf_op jit(solution)/shard_map/ppermute | solution.py:31
  670.0 4.0 copy.172
  674.0 3.9 copy.163
  683.7 4.6 convolution_bitcast_fusion.3
  688.3 5.3 copy.156
  696.2 6.0 fusion.42
  702.2 4.0 convolution_bitcast_fusion.2
  706.3 5.2 copy.165
  711.5 15.1 %collective-permute-done.11 = bf16[8,4,128,128]{3,1,2,0:T(4,128)(2,1)} collective-permute-done((bf16[8,4,128,128]{3,1,2,0:T(4,128)(2,1)}, bf16[8,4,128,128]{3,1,2,0:T(4,128)(2,1)}, u32[]{:S(2)}, u32[]{:S(2)}) %collective-permute-start.11) | collective-permute-done | bytes 1048608 | tf_op jit(solution)/shard_map/ppermute | solution.py:31
  728.5 7.2 fusion.40
  735.6 4.0 convolution_bitcast_fusion.1
  739.6 5.4 copy.174
  745.1 7.4 fusion.38
  752.5 14.8 %collective-permute-done.13 = bf16[8,4,128,128]{3,1,2,0:T(4,128)(2,1)S(1)} collective-permute-done((bf16[8,4,128,128]{3,1,2,0:T(4,128)(2,1)}, bf16[8,4,128,128]{3,1,2,0:T(4,128)(2,1)S(1)}, u32[]{:S(2)}, u32[]{:S(2)}) %collective-permute-start.13) | collective-permute-done | bytes 1048608 | tf_op jit(solution)/shard_map/ppermute | solution.py:31
  770.0 5.2 copy.183
  775.2 8.3 %fusion.12 = bf16[8,1,4,128,128]{4,2,3,0,1:T(4,128)(2,1)S(1)} fusion(f32[8,4,2,128,128]{4,1,2,3,0:T(4,128)} %copy.183, f32[8,4,128,128,1]{3,1,4,2,0:T(4,128)} %fusion.38, f32[8,4,128,128,1]{3,1,4,2,0:T(4,128)} %fusion.40, f32[8,4,128,128,1]{3,1,4,2,0:T(4,128)S(1)} %fusion.42, bf16[8,4,128,128]{3,1,2,0:T(4,128)(2,1)} %fusion.3, s32[8,4,2]{1,2,0:T(2,128)S(1)} %copy.178, ...), kind=kOutput, calls=%fused_computation.42 | convolution fusion | flops 54526208 | bytes 12583296 | tf_op jit(solution)/shard_map/aijt,aijxz->atxz/dot_general | solution.py:41
  (146 shorter events, 86.4 us)
Async XLA Ops:
  6.5 540.6 %all-reduce.4.cloned.1.call-start = ((), (), s32[]{:S(2)}) async-start(), calls=%async_computation | async-start | bytes 8388608 | tf_op jit(solution)/shard_map/psum | solution.py:17
  6.5 34.4 %collective-permute-start.1 = (bf16[8,2,128,128]{3,2,1,0:T(8,128)(2,1)}, bf16[8,2,128,128]{3,2,1,0:T(8,128)(2,1)S(1)}, u32[]{:S(2)}, u32[]{:S(2)}) collective-permute-start(bf16[8,2,128,128]{3,2,1,0:T(8,128)(2,1)} %bitcast.171), channel_id=1, source_target_pairs={{0,16},{16,32},{32,48},{48,64},{64,80},{80,96},{96,112},{112,128},... | collective-permute-start | bytes 1572872 | tf_op jit(solution)/shard_map/ppermute | solution.py:12
  10.9 303.3 %collective-permute-start.3 = (bf16[8,2,128,128]{3,2,1,0:T(8,128)(2,1)}, bf16[8,2,128,128]{3,2,1,0:T(8,128)(2,1)S(1)}, u32[]{:S(2)}, u32[]{:S(2)}) collective-permute-start(bf16[8,2,128,128]{3,2,1,0:T(8,128)(2,1)} %bitcast.172), channel_id=1, source_target_pairs={{0,15},{1,0},{2,1},{3,2},{4,3},{5,4},{6,5},{7,6},{8,7},{9,8},{10,9... | collective-permute-start | bytes 1572872 | tf_op jit(solution)/shard_map/ppermute | solution.py:31
  16.7 40.7 %collective-permute-start.2 = (s32[8,2]{0,1:T(2,128)}, s32[8,2]{0,1:T(2,128)S(1)}, u32[]{:S(2)}, u32[]{:S(2)}) collective-permute-start(s32[8,2]{0,1:T(2,128)} %bitcast.185), channel_id=1, source_target_pairs={{0,15},{1,0},{2,1},{3,2},{4,3},{5,4},{6,5},{7,6},{8,7},{9,8},{10,9... | collective-permute-start | bytes 200 | tf_op jit(solution)/shard_map/ppermute | solution.py:31
  30.3 9.9 %collective-permute-start = (s32[8,2]{0,1:T(2,128)}, s32[8,2]{0,1:T(2,128)S(1)}, u32[]{:S(2)}, u32[]{:S(2)}) collective-permute-start(s32[8,2]{0,1:T(2,128)} %bitcast.186), channel_id=1, source_target_pairs={{0,16},{16,32},{32,48},{48,64},{64,80},{80,96},{96,112},{112,128},... | collective-permute-start | bytes 200 | tf_op jit(solution)/shard_map/ppermute | solution.py:12
  32.9 264.5 %collective-permute-start.8 = (s32[8,4]{0,1:T(4,128)}, s32[8,4]{0,1:T(4,128)S(1)}, u32[]{:S(2)}, u32[]{:S(2)}) collective-permute-start(s32[8,4]{0,1:T(4,128)} %bitcast.183), channel_id=1, source_target_pairs={{0,15},{1,0},{2,1},{3,2},{4,3},{5,4},{6,5},{7,6},{8,7},{9,8},{10,9... | collective-permute-start | bytes 392 | tf_op jit(solution)/shard_map/ppermute | solution.py:31
  265.9 30.4 %collective-permute-start.4 = (s32[8,2]{0,1:T(2,128)S(1)}, s32[8,2]{0,1:T(2,128)S(1)}, u32[]{:S(2)}, u32[]{:S(2)}) collective-permute-start(s32[8,2]{0,1:T(2,128)S(1)} %collective-permute-done.2), channel_id=1, source_target_pairs={{0,15},{1,0},{2,1},{3,2},{4,3},{5,4},{6,5},{7,6},{8,7},{9,8},{10,9... | collective-permute-start | bytes 200 | tf_op jit(solution)/shard_map/ppermute | solution.py:31
  298.4 14.8 %collective-permute-start.6 = (s32[8,2]{0,1:T(2,128)S(1)}, s32[8,2]{0,1:T(2,128)S(1)}, u32[]{:S(2)}, u32[]{:S(2)}) collective-permute-start(s32[8,2]{0,1:T(2,128)S(1)} %collective-permute-done.4), channel_id=1, source_target_pairs={{0,15},{1,0},{2,1},{3,2},{4,3},{5,4},{6,5},{7,6},{8,7},{9,8},{10,9... | collective-permute-start | bytes 200 | tf_op jit(solution)/shard_map/ppermute | solution.py:31
  300.4 15.9 %collective-permute-start.10 = (s32[8,4]{0,1:T(4,128)S(1)}, s32[8,4]{0,1:T(4,128)S(1)}, u32[]{:S(2)}, u32[]{:S(2)}) collective-permute-start(s32[8,4]{0,1:T(4,128)S(1)} %collective-permute-done.8), channel_id=1, source_target_pairs={{0,15},{1,0},{2,1},{3,2},{4,3},{5,4},{6,5},{7,6},{8,7},{9,8},{10,9... | collective-permute-start | bytes 392 | tf_op jit(solution)/shard_map/ppermute | solution.py:31
  314.2 232.9 %copy-start.9 = (bf16[8,2,128,128]{3,2,1,0:T(8,128)(2,1)}, bf16[8,2,128,128]{3,2,1,0:T(8,128)(2,1)S(1)}, u32[]{:S(2)}) copy-start(bf16[8,2,128,128]{3,2,1,0:T(8,128)(2,1)S(1)} %collective-permute-done.3) | copy-start | bytes 1572868
  314.2 35.3 %collective-permute-start.5 = (bf16[8,2,128,128]{3,2,1,0:T(8,128)(2,1)S(1)}, bf16[8,2,128,128]{3,2,1,0:T(8,128)(2,1)}, u32[]{:S(2)}, u32[]{:S(2)}) collective-permute-start(bf16[8,2,128,128]{3,2,1,0:T(8,128)(2,1)S(1)} %collective-permute-done.3), channel_id=1, source_target_pairs={{0,15},{1,0},{2,1},{3,2},{4,3},{5,4},{6,5},{7,6},{8,7},{9,8},{10,9... | collective-permute-start | bytes 1572872 | tf_op jit(solution)/shard_map/ppermute | solution.py:31
  349.5 226.1 %collective-permute-start.7 = (bf16[8,2,128,128]{3,2,1,0:T(8,128)(2,1)}, bf16[8,2,128,128]{3,2,1,0:T(8,128)(2,1)}, u32[]{:S(2)}, u32[]{:S(2)}) collective-permute-start(bf16[8,2,128,128]{3,2,1,0:T(8,128)(2,1)} %collective-permute-done.5), channel_id=1, source_target_pairs={{0,15},{1,0},{2,1},{3,2},{4,3},{5,4},{6,5},{7,6},{8,7},{9,8},{10,9... | collective-permute-start | bytes 1572872 | tf_op jit(solution)/shard_map/ppermute | solution.py:31
  551.3 2.4 copy-start.2
  558.0 4.2 copy-start.1
  567.5 4.2 copy-start
  583.1 5.1 copy-start.6
  588.2 3.9 copy-start.7
  592.1 3.9 copy-start.8
  601.4 80.4 %collective-permute-start.9 = (bf16[8,4,128,128]{3,1,2,0:T(4,128)(2,1)}, bf16[8,4,128,128]{3,1,2,0:T(4,128)(2,1)}, u32[]{:S(2)}, u32[]{:S(2)}) collective-permute-start(bf16[8,4,128,128]{3,1,2,0:T(4,128)(2,1)} %fusion.3), channel_id=1, source_target_pairs={{0,15},{1,0},{2,1},{3,2},{4,3},{5,4},{6,5},{7,6},{8,7},{9,8},{10,9... | collective-permute-start | bytes 3145736 | tf_op jit(solution)/shard_map/ppermute | solution.py:31
  624.9 35.5 %collective-permute-start.12 = (s32[8,4]{0,1:T(4,128)S(1)}, s32[8,4]{0,1:T(4,128)S(1)}, u32[]{:S(2)}, u32[]{:S(2)}) collective-permute-start(s32[8,4]{0,1:T(4,128)S(1)} %collective-permute-done.10), channel_id=1, source_target_pairs={{0,15},{1,0},{2,1},{3,2},{4,3},{5,4},{6,5},{7,6},{8,7},{9,8},{10,9... | collective-permute-start | bytes 392 | tf_op jit(solution)/shard_map/ppermute | solution.py:31
  681.8 44.8 %collective-permute-start.11 = (bf16[8,4,128,128]{3,1,2,0:T(4,128)(2,1)}, bf16[8,4,128,128]{3,1,2,0:T(4,128)(2,1)}, u32[]{:S(2)}, u32[]{:S(2)}) collective-permute-start(bf16[8,4,128,128]{3,1,2,0:T(4,128)(2,1)} %collective-permute-done.9), channel_id=1, source_target_pairs={{0,15},{1,0},{2,1},{3,2},{4,3},{5,4},{6,5},{7,6},{8,7},{9,8},{10,9... | collective-permute-start | bytes 3145736 | tf_op jit(solution)/shard_map/ppermute | solution.py:31
  696.2 6.0 copy-start.5
  711.5 24.2 %copy-start.3 = (bf16[8,4,2,128,128]{3,4,2,1,0:T(8,128)(2,1)S(1)}, bf16[8,4,2,128,128]{3,4,2,1,0:T(8,128)(2,1)}, u32[]{:S(2)}) copy-start(bf16[8,4,2,128,128]{3,4,2,1,0:T(8,128)(2,1)} %copy.172) | copy-start | bytes 6291460
  726.6 40.7 %collective-permute-start.13 = (bf16[8,4,128,128]{3,1,2,0:T(4,128)(2,1)}, bf16[8,4,128,128]{3,1,2,0:T(4,128)(2,1)S(1)}, u32[]{:S(2)}, u32[]{:S(2)}) collective-permute-start(bf16[8,4,128,128]{3,1,2,0:T(4,128)(2,1)} %collective-permute-done.11), channel_id=1, source_target_pairs={{0,15},{1,0},{2,1},{3,2},{4,3},{5,4},{6,5},{7,6},{8,7},{9,8},{10,9... | collective-permute-start | bytes 3145736 | tf_op jit(solution)/shard_map/ppermute | solution.py:31
  745.1 22.2 %copy-start.4 = (bf16[8,4,2,128,128]{3,4,2,1,0:T(8,128)(2,1)S(1)}, bf16[8,4,2,128,128]{3,4,2,1,0:T(8,128)(2,1)}, u32[]{:S(2)}) copy-start(bf16[8,4,2,128,128]{3,4,2,1,0:T(8,128)(2,1)} %copy.181) | copy-start | bytes 6291460
Sparse Core Ops, SparseCore 0:
  44.3 502.7 all-reduce.3
where the time goes:
time: 796 us; the launch traced here: 792 us
  waiting for transfers between devices  312 us (39%)
  blocking collectives  206 us (26%)
  starting transfers between devices  99.9 us (13%)
  local copies, waits for them, and re-layouts  79.6 us (10%)
  matrix products  73.4 us (9%)
  between operations  14 us (2%)
    psum x1, blocking collectives, broadcast(): return lax.psum(jnp.where(mine, array, jnp.zeros_like(array)), axis)  206 us
    psum x1, waiting for transfers between devices, broadcast(): return lax.psum(jnp.where(mine, array, jnp.zeros_like(array)), axis)  195 us
    ppermute x12, waiting for transfers between devices, shifted_2(): return lax.ppermute(value, axis, pairs)  117 us
    ppermute x12, starting transfers between devices, shifted_2(): return lax.ppermute(value, axis, pairs)  92.8 us
    dot_general x8, matrix products, section_terms(): jnp.einsum('aijt,aijxz->atxz', matches, products, precision=lax.Precision...  47.2 us
    transpose x8, local copies, waits for them, and re-layouts, section_terms(): jnp.einsum('aixy,aijyz->aijxz', left_blocks, picked, preferred_element_ty...  36.1 us
    gather x16, local copies, waits for them, and re-layouts, section_terms(): picked = jnp.take(right_blocks, left_index, axis=0)  33 us
    dot_general x8, matrix products, section_terms(): jnp.einsum('aixy,aijyz->aijxz', left_blocks, picked, preferred_element_ty...  26.2 us
  transfers between devices with their start and end apart: 15, of which 8 were waited for; matrix products, arithmetic and copies ran while one was open for 15% of the time, Pallas kernels for 0%

commit v1 on v0

v1 whole, which is shorter than its diff:
```python
import functools

import jax
import jax.numpy as jnp
from jax import lax
from jax.experimental import pallas as pl
from jax.experimental.pallas import tpu as pltpu
from jax.sharding import PartitionSpec as P

MESH = pl.DeviceIdType.MESH
ROWS, COLS = 32, 16
NX, NZ = 4, 8
BS = 128
META = 48
ZERO = 128


def place():
    r, c = lax.axis_index("row"), lax.axis_index("col")
    return r, c, r // NZ, r % NZ, c % 2


def remote(src, dst, send, recv, device):
    return pltpu.make_async_remote_copy(
        src_ref=src, dst_ref=dst, send_sem=send, recv_sem=recv, device_id=device, device_id_type=MESH
    )


def gather_kernel(
    d, left, right, s_scat, r_scat, s_z, r_z, s_x, r_x, s_h, r_h, s_cross, r_cross, s_left, r_left, local
):
    r, c, x, z, kap = place()
    sib = c + 1 - 2 * kap
    xr, xl, xo = (x + 1) % NX, (x + 3) % NX, (x + 2) % NX
    up, down = z < NZ - 1, z > 0
    source = ((r - 2 * c + ROWS) % ROWS < 8, (r - 2 * c - 4 + 2 * ROWS) % ROWS < 8)
    back2, back3, back4 = (c + 14) % COLS, (c + 13) % COLS, (c + 12) % COLS
    third = (c + jnp.where(kap == 0, 13, 3)) % COLS

    barrier = pltpu.get_barrier_semaphore()

    def greet(device):
        pl.semaphore_signal(barrier, inc=1, device_id=device, device_id_type=MESH)

    for column in (back2, (c + 2) % COLS, back4, (c + 4) % COLS, sib, third):
        greet((r, column))
    for other in (xr, xl, xo):
        greet((other * NZ + z, c))

    @pl.when(up)
    def _():
        greet((r + 1, c))

    @pl.when(down)
    def _():
        greet((r - 1, c))

    pl.semaphore_wait(barrier, 9 + up.astype(jnp.int32) + down.astype(jnp.int32))

    def cross(u):
        part = pl.ds(4 * u, 4)
        return remote(d.at[part], left.at[1, part], s_cross.at[u], r_cross.at[u], (r, back2))

    def scatter(tile, step):
        other = (x + step) % NX
        part = pl.ds(4 * other, 4)
        src = d if tile == 0 else left.at[1]
        return remote(
            src.at[part], right.at[tile, z, part], s_scat.at[tile, step - 1], r_scat.at[tile], (other * NZ + z, c)
        )

    def keep(tile):
        part = pl.ds(4 * x, 4)
        src = d if tile == 0 else left.at[1]
        return pltpu.make_async_copy(src.at[part], right.at[tile, z, part], local.at[tile])

    def along_z(tile, piece, way):
        part = right.at[tile, piece, pl.ds(4 * x, 4)]
        to = r + 1 if way == 0 else r - 1
        return remote(part, part, s_z.at[tile, piece, way], r_z.at[tile, piece], (to, c))

    def along_x(tile, piece, way):
        part = right.at[tile, piece, pl.ds(4 * x, 4)]
        to = xr if way == 0 else xl
        return remote(part, part, s_x.at[tile, piece, way], r_x.at[tile, piece, way], (to * NZ + z, c))

    def came_x(tile, piece, way):
        part = right.at[tile, piece, pl.ds(4 * (xl if way == 0 else xr), 4)]
        return remote(part, part, s_x.at[tile, piece, way], r_x.at[tile, piece, way], (r, c))

    def half_x(tile, piece, way):
        part = right.at[tile, piece, pl.ds(4 * xl if way == 0 else 4 * xr + 2, 2)]
        to = xr if way == 0 else xl
        return remote(part, part, s_h.at[tile, piece, way], r_h.at[tile, piece, way], (to * NZ + z, c))

    def came_half(tile, piece, way):
        part = right.at[tile, piece, pl.ds(4 * xo + 2 * way, 2)]
        return remote(part, part, s_h.at[tile, piece, way], r_h.at[tile, piece, way], (r, c))

    def begin(tile):
        @pl.when(source[tile])
        def _():
            keep(tile).wait()

        @pl.when(jnp.logical_not(source[tile]))
        def _():
            part = right.at[tile, z, pl.ds(4 * x, 4)]
            remote(part, part, s_scat.at[tile, 0], r_scat.at[tile], (r, c)).wait_recv()

        @pl.when(up)
        def _():
            along_z(tile, z, 0).start()

        @pl.when(down)
        def _():
            along_z(tile, z, 1).start()

        along_x(tile, z, 0).start()
        along_x(tile, z, 1).start()

    def z_step(tile, step):
        for way in (0, 1):
            piece = z - step if way == 0 else z + step
            onward = up if way == 0 else down

            @pl.when(piece >= 0 if way == 0 else piece < NZ)
            def _():
                along_z(tile, piece, way).wait_recv()

                @pl.when(onward)
                def _():
                    along_z(tile, piece, way).start()

                along_x(tile, piece, 0).start()
                along_x(tile, piece, 1).start()

    def x_step(tile, piece):
        for way in (0, 1):
            came_x(tile, piece, way).wait_recv()
            half_x(tile, piece, way).start()

    def x_round(tile, step):
        for way in (0, 1):
            piece = z - step if way == 0 else z + step

            @pl.when(piece >= 0 if way == 0 else piece < NZ)
            def _():
                x_step(tile, piece)

    def begin_cross():
        for u in range(4):
            cross(u).start()

    def end_cross():
        for u in range(4):
            cross(u).wait_recv()

    def send_y():
        return remote(d, left.at[3], s_left.at[0], r_left.at[3], (r, back4))

    def send_own():
        return remote(d, left.at[0], s_left.at[1], r_left.at[0], (r, sib))

    def pass_cross():
        return remote(left.at[1], left.at[2 * kap], s_left.at[2], r_left.at[2 * kap], (r, sib))

    def pass_cross_y():
        return remote(left.at[1], left.at[4], s_left.at[3], r_left.at[4], (r, back3))

    def pass_y():
        return remote(left.at[3], left.at[2 + 2 * kap], s_left.at[4], r_left.at[2 + 2 * kap], (r, sib))

    @pl.when(source[0])
    def _():
        keep(0).start()
        begin_cross()
        for step in (1, 2, 3):
            scatter(0, step).start()

    send_y().start()

    @pl.when(kap == 1)
    def _():
        send_own().start()

    begin(0)
    z_step(0, 1)

    @pl.when(jnp.logical_not(source[0]))
    def _():
        begin_cross()

    z_step(0, 2)
    z_step(0, 3)

    @pl.when(source[1])
    def _():
        end_cross()
        keep(1).start()
        for step in (1, 2, 3):
            scatter(1, step).start()

    @pl.loop(4, NZ)
    def _(step):
        z_step(0, step)

    send_y().wait_recv()
    pass_y().start()
    begin(1)
    x_step(0, z)

    @pl.loop(1, NZ)
    def _(step):
        z_step(1, step)
        x_round(0, step)

    @pl.when(jnp.logical_not(source[1]))
    def _():
        end_cross()

    pass_cross().start()

    @pl.when(kap == 0)
    def _():
        pass_cross_y().start()

    x_step(1, z)

    @pl.loop(1, NZ)
    def _(step):
        x_round(1, step)

    @pl.loop(0, NZ)
    def _(piece):
        for tile in (0, 1):
            for way in (0, 1):
                came_half(tile, piece, way).wait_recv()
                along_x(tile, piece, way).wait_send()
                half_x(tile, piece, way).wait_send()

            @pl.when(jnp.logical_and(up, piece <= z))
            def _():
                along_z(tile, piece, 0).wait_send()

            @pl.when(jnp.logical_and(down, piece >= z))
            def _():
                along_z(tile, piece, 1).wait_send()

    for slot in (0, 2, 4):
        remote(left.at[slot], left.at[slot], s_left.at[0], r_left.at[slot], (r, c)).wait_recv()
    for u in range(4):
        cross(u).wait_send()
    for tile in (0, 1):

        @pl.when(source[tile])
        def _():
            for step in (1, 2, 3):
                scatter(tile, step).wait_send()

    send_y().wait_send()
    pass_cross().wait_send()
    pass_y().wait_send()

    @pl.when(kap == 1)
    def _():
        send_own().wait_send()

    @pl.when(kap == 0)
    def _():
        pass_cross_y().wait_send()


def product_kernel(meta, d, left, right, out, lv, rv0, rv1, sv, acc, loads, s_sq, r_sq):
    r, c, x, z, kap = place()
    sib = c + 1 - 2 * kap
    back3 = (c + 13) % COLS
    third = (c + jnp.where(kap == 0, 13, 3)) % COLS
    barrier = pltpu.get_barrier_semaphore()
    for column in (sib, third):
        pl.semaphore_signal(barrier, inc=1, device_id=(r, column), device_id_type=MESH)

    copies = [
        pltpu.make_async_copy(d, lv.at[0], loads.at[0]),
        pltpu.make_async_copy(left, lv.at[pl.ds(1, 5)], loads.at[1]),
        pltpu.make_async_copy(right.at[pl.ds(0, 128)], rv0.at[pl.ds(0, 128)], loads.at[2]),
        pltpu.make_async_copy(right.at[pl.ds(128, 128)], rv1.at[pl.ds(0, 128)], loads.at[3]),
    ]
    for copy in copies:
        copy.start()
    for rv in (rv0, rv1):
        rv[ZERO] = jnp.zeros((BS, BS), jnp.bfloat16)
    pl.semaphore_wait(barrier, 2)

    def picks(tile, section, inner, kept):
        column = (c + 2 * tile) % COLS
        group = (2 * column + 2 * section + (inner >> 3)) % ROWS
        row = 2 * (inner & 7)
        at = (group * COLS + column) * META + row
        first, second = meta[at], meta[at + 1]
        base = (group % NZ) * 16 + row
        return [
            jnp.where(first == wanted, base, jnp.where(second == wanted, base + 1, ZERO)) for wanted in kept
        ]

    def kept_of(column, a):
        at = (r * COLS + column) * META + 16 + 4 * a
        return [meta[at + t] for t in range(4)]

    def terms(total, lefts, rv, spots):
        lhs = jnp.concatenate(lefts, axis=1)
        parts = []
        for pair in (0, 2):
            rhs = jnp.concatenate(
                [jnp.concatenate([rv[spot[pair]], rv[spot[pair + 1]]], axis=1) for spot in spots], axis=0
            )
            parts.append(jnp.dot(lhs, rhs, preferred_element_type=jnp.float32))
        return parts if total is None else [old + new for old, new in zip(total, parts)]

    def send(tile, a):
        slot = jnp.where(kap == 0, 3 - 2 * tile, 1 + 2 * tile)
        to = sib if tile == 1 else jnp.where(kap == 0, back3, sib)
        rows = pl.ds(4 * a, 4)
        return remote(
            sv.at[2 * tile, rows], sv.at[slot, rows], s_sq.at[tile, a], r_sq.at[slot, a], (r, to)
        )

    def came(slot, a):
        rows = pl.ds(4 * a, 4)
        return remote(sv.at[slot, rows], sv.at[slot, rows], s_sq.at[0, a], r_sq.at[slot, a], (r, c))

    def square(tile, a):
        kept = kept_of((c + 2 * tile) % COLS, a)
        total = None
        for section in range(4):
            owner = (r * COLS + (c + 2 * tile + section) % COLS) * META + 2 * a
            spots = [picks(tile, section, meta[owner + i], kept) for i in range(2)]
            total = terms(total, [lv[2 * tile + section, 2 * a + i] for i in range(2)], rv1 if tile else rv0, spots)
        for t in range(4):
            sv[2 * tile, 4 * a + t] = total[t // 2][:, (t % 2) * BS : (t % 2 + 1) * BS].astype(jnp.bfloat16)
        send(tile, a).start()

    def cube(sections, a, total):
        kept = kept_of(c, a)
        for section in sections:
            inner = kept_of((c + section) % COLS, a)
            for i in (0, 2):
                spots = [picks(0, section, inner[i + e], kept) for e in range(2)]
                total = terms(total, [sv[section, 4 * a + i + e] for e in range(2)], rv0, spots)
        return total

    copies[0].wait()
    copies[1].wait()
    copies[2].wait()

    @pl.loop(0, 8)
    def _(a):
        square(0, a)

    copies[3].wait()

    @pl.loop(0, 8)
    def _(a):
        square(1, a)

    @pl.loop(0, 8)
    def _(a):
        total = cube((0, 2), a, None)
        acc[a, 0] = total[0]
        acc[a, 1] = total[1]

    @pl.loop(0, 8)
    def _(a):
        came(1, a).wait_recv()
        came(3, a).wait_recv()
        total = cube((1, 3), a, [acc[a, 0], acc[a, 1]])
        for t in range(4):
            part = total[t // 2][:, (t % 2) * BS : (t % 2 + 1) * BS]
            out[4 * a + t] = (3.0 * sv[0, 4 * a + t].astype(jnp.float32) - 2.0 * part).astype(jnp.bfloat16)

    @pl.loop(0, 8)
    def _(a):
        send(0, a).wait_send()
        send(1, a).wait_send()


def on_device(density, pattern, kept_pattern):
    own = density.reshape(16, BS, BS)
    meta = jnp.concatenate([pattern.reshape(16), kept_pattern.reshape(32)])
    meta = lax.all_gather(meta, ("row", "col"), tiled=True)
    dma = pltpu.SemaphoreType.DMA
    left, right = pl.pallas_call(
        gather_kernel,
        out_shape=(
            jax.ShapeDtypeStruct((5, 16, BS, BS), jnp.bfloat16),
            jax.ShapeDtypeStruct((2, NZ, 16, BS, BS), jnp.bfloat16),
        ),
        in_specs=[pl.BlockSpec(memory_space=pl.ANY)],
        out_specs=(pl.BlockSpec(memory_space=pl.ANY),) * 2,
        scratch_shapes=[
            dma((2, 3)),
            dma((2,)),
            dma((2, NZ, 2)),
            dma((2, NZ)),
            dma((2, NZ, 2)),
            dma((2, NZ, 2)),
            dma((2, NZ, 2)),
            dma((2, NZ, 2)),
            dma((4,)),
            dma((4,)),
            dma((5,)),
            dma((5,)),
            dma((2,)),
        ],
        compiler_params=pltpu.CompilerParams(collective_id=0, has_side_effects=True),
        cost_estimate=pl.CostEstimate(flops=0, bytes_accessed=300 << 20, transcendentals=0),
        name="gather_blocks",
    )(own)
    out = pl.pallas_call(
        product_kernel,
        out_shape=jax.ShapeDtypeStruct((32, BS, BS), jnp.bfloat16),
        in_specs=[pl.BlockSpec(memory_space=pltpu.SMEM)] + [pl.BlockSpec(memory_space=pl.ANY)] * 3,
        out_specs=pl.BlockSpec(memory_space=pltpu.VMEM),
        scratch_shapes=[
            pltpu.VMEM((6, 16, BS, BS), jnp.bfloat16),
            pltpu.VMEM((ZERO + 1, BS, BS), jnp.bfloat16),
            pltpu.VMEM((ZERO + 1, BS, BS), jnp.bfloat16),
            pltpu.VMEM((4, 32, BS, BS), jnp.bfloat16),
            pltpu.VMEM((8, 2, BS, 2 * BS), jnp.float32),
            dma((4,)),
            dma((2, 8)),
            dma((4, 8)),
        ],
        compiler_params=pltpu.CompilerParams(
            collective_id=1, has_side_effects=True, vmem_limit_bytes=40 << 20
        ),
        cost_estimate=pl.CostEstimate(flops=4 << 30, bytes_accessed=12 << 20, transcendentals=0),
        name="square_and_cube",
    )(meta, own, left, right.reshape(256, BS, BS))
    return out.reshape(8, 1, 4, BS, BS)


def solution(mesh):
    in_specs = (P("row", "col", None, None, None), P("row", "col", None), P("row", "col", None))
    out_specs = P("row", "col", None, None, None)
    return jax.shard_map(
        on_device, mesh=mesh, in_specs=in_specs, out_specs=out_specs, check_vma=False
    )
```

time: 796 us -> 526 us (0.66)
  blocking collectives: 206 us -> 0 us
  Pallas kernels: 0 us -> 167 us
  starting transfers between devices: 99.9 us -> 0.01 us
  matrix products: 73.4 us -> 0 us
  local copies, waits for them, and re-layouts: 79.6 us -> 10.3 us
  waiting for transfers between devices: 312 us -> 334 us
    unnamed x1 -> x2, waiting for transfers between devices: 0.02 us -> 334 us
    psum x1 -> x0, blocking collectives: 206 us -> none  [broadcast(): return lax.psum(jnp.where(mine, array, jnp.zeros_like(array)), axis)]
    psum x1 -> x0, waiting for transfers between devices: 195 us -> none  [broadcast(): return lax.psum(jnp.where(mine, array, jnp.zeros_like(array)), axis)]
    pallas_call x0 -> x2, Pallas kernels: none -> 167 us  [the longest x1 148 us: on_device(): pl.pallas_call(gather_kernel, out_shape=(jax.ShapeDtypeStruct((5, 16, BS,...]
    ppermute x14 -> x0, waiting for transfers between devices: 117 us -> none  [the longest x12 117 us: shifted_2(): return lax.ppermute(value, axis, pairs)]
    ppermute x14 -> x0, starting transfers between devices: 99.8 us -> none  [the longest x12 92.8 us: shifted_2(): return lax.ppermute(value, axis, pairs)]
    dot_general x16 -> x0, matrix products: 73.4 us -> none  [the longest x8 47.2 us: section_terms(): jnp.einsum('aijt,aijxz->atxz', matches, products, precision=lax.Precision...]
    gather x32 -> x0, local copies, waits for them, and re-layouts: 38.6 us -> none  [the longest x16 33 us: section_terms(): picked = jnp.take(right_blocks, left_index, axis=0)]
  transfers between devices with their start and end apart: 15 -> 1, of which waited for: 8 -> 1; matrix products, arithmetic and copies ran while one was open for 15% -> 0% of each run, Pallas kernels for 0% -> 28%
where the time goes in v1:
time: 526 us; the launch traced here: 525 us
  waiting for transfers between devices  334 us (63%)
  Pallas kernels  167 us (32%)
  between operations  13.4 us (3%)
  local copies, waits for them, and re-layouts  10.3 us (2%)
    unnamed x2, waiting for transfers between devices  334 us
    pallas_call x1, Pallas kernels, on_device(): pl.pallas_call(gather_kernel, out_shape=(jax.ShapeDtypeStruct((5, 16, BS,...  148 us
    pallas_call x1, Pallas kernels, on_device(): pl.pallas_call(product_kernel, out_shape=jax.ShapeDtypeStruct((32, BS, BS...  19.5 us
  transfers between devices with their start and end apart: 1, of which 1 were waited for; matrix products, arithmetic and copies ran while one was open for 0% of the time, Pallas kernels for 28%

profile of v1, /device:TPU:1, one launch (start us, length us, event | category | flops | bytes accessed | tf_op | source)
XLA Modules:
  0.0 525.2 jit_solution(9447124107734084350)
XLA Ops:
  6.5 0.0 all-reduce.3.cloned.1.call-start
  6.5 0.8 copy.7
  7.3 0.1 reshape.15
  7.4 0.8 copy.8
  8.1 0.1 reshape.16
  8.2 0.2 add_dynamic-update-slice_fusion
  8.4 0.0 copy-start.4
  8.4 0.6 copy-done.4
  9.1 0.0 all-reduce.3.cloned.1.call-update
  9.1 147.7 %gather_blocks.1 = (bf16[5,16,128,128]{3,2,1,0:T(8,128)(2,1)}, bf16[2,8,16,128,128]{4,3,2,1,0:T(8,128)(2,1)}) custom-call(bf16[16,128,128]{2,1,0:T(8,128)(2,1)} %bitcast.10), custom_call_target="tpu_custom_call" | custom-call | bytes 314572800 | tf_op jit(solution)/shard_map/gather_blocks/pallas_call | solution.py:391
  156.8 334.0 %all-reduce.3.cloned.1.call-done.meta = s32[24576]{0:T(1024)} async-done(((s32[24576]{0:T(1024)}), s32[24576]{0:T(1024)}) %all-reduce.3.cloned.1.call-update) | async-done | bytes 98320
  490.8 0.0 copy-start
  490.8 1.0 copy-done
  491.9 0.0 copy-start.1
  491.9 3.4 copy-done.1
  495.3 0.0 copy-start.2
  495.3 1.7 copy-done.2
  497.0 0.0 copy-start.3
  497.0 0.9 copy-done.3
  497.9 19.5 %square_and_cube.1 = bf16[32,128,128]{2,1,0:T(8,128)(2,1)S(1)} custom-call(s32[24576]{0:T(1024)S(1)} %copy-done.3, bf16[16,128,128]{2,1,0:T(8,128)(2,1)S(1)} %bitcast.11, bf16[5,16,128,128]{3,2,1,0:T(8,128)(2,1)S(1)} %copy-done.2, bf16[256,128,128]{2,1,0:T(8,128)(2,1)S(1)} %bitcast.12), custom_call_target="tpu_custom_call" | custom-call | flops 4294967296 | bytes 12582912 | tf_op jit(solution)/shard_map/square_and_cube/pallas_call | solution.py:418
  517.4 1.0 copy.13
  (1 shorter events, 0.0 us)
Async XLA Ops:
  6.5 484.3 %all-reduce.3.cloned.1.call-start = ((), (), s32[]{:S(2)}) async-start(), calls=%async_computation | async-start | bytes 196608
  8.4 0.6 copy-start.4
  490.8 1.0 copy-start
  491.9 3.4 copy-start.1
  495.3 1.7 copy-start.2
  497.0 0.9 copy-start.3
Sparse Core Ops, SparseCore 0:
  12.8 477.9 all-reduce.2

commit v2 on v0

v2 whole, which is shorter than its diff:
```python
import jax
import jax.numpy as jnp
from jax import lax
from jax.experimental import pallas as pl
from jax.experimental.pallas import tpu as pltpu
from jax.sharding import PartitionSpec as P

MESH = pl.DeviceIdType.MESH
ROWS, COLS = 32, 16
NX, NZ = 4, 8
BS = 128
ZERO = 128
LAG = 2
CROSS_AT = (0, 0, 0, 0)
PARTS = 3


def remote(src, dst, send, recv, device):
    return pltpu.make_async_remote_copy(
        src_ref=src, dst_ref=dst, send_sem=send, recv_sem=recv, device_id=device, device_id_type=MESH
    )


def kernel(
    meta, d, out,
    left, rv0, rv1, sv, acc, ml, m0, m1, tl, t0, t1,
    s_sc, s_scm, r_sc, local,
    s_z, r_z, s_zm, r_zm,
    s_a, r_a, s_b, r_b, s_am, r_am,
    s_x0, r_x0, s_h0, r_h0, s_x1, r_x1, s_h1, r_h1,
    s_cr, r_cr, s_l, r_l, s_ml, r_ml, s_sq, r_sq,
):
    r, c = lax.axis_index("row"), lax.axis_index("col")
    x, z, kap = r // NZ, r % NZ, c % 2
    sib = c + 1 - 2 * kap
    xr, xl, xo = (x + 1) % NX, (x + 3) % NX, (x + 2) % NX
    up, down = z < NZ - 1, z > 0
    source = (r - 2 * c + ROWS) % ROWS < NZ
    edge = x * NZ + NZ - 1 - z

    def back(steps):
        return (c + COLS - steps) % COLS

    barrier = pltpu.get_barrier_semaphore()

    def greet(device):
        pl.semaphore_signal(barrier, inc=1, device_id=device, device_id_type=MESH)

    for steps in range(1, 6):
        greet((r, back(steps)))
        greet((r, (c + steps) % COLS))
    for other in (xr, xl, xo):
        greet((other * NZ + z, c))

    @pl.when(up)
    def _():
        greet((r + 1, c))

    @pl.when(down)
    def _():
        greet((r - 1, c))

    @pl.when(jnp.logical_not(jnp.logical_and(up, down)))
    def _():
        greet((edge, back(2)))
        greet((edge, (c + 2) % COLS))

    inside = jnp.logical_and(up, down)
    pl.semaphore_wait(barrier, jnp.where(inside, 15, 16))


    def quarter(buffer, piece, which, start=0, size=4):
        return buffer.at[pl.ds(piece * 16 + 4 * which + start, size)]

    def scatter(step):
        other = (x + step) % NX
        to = (other * NZ + z, c)
        return (
            remote(d.at[pl.ds(4 * other, 4)], quarter(rv0, z, other), s_sc.at[step - 1], r_sc.at[0], to),
            remote(meta, m0.at[z], s_scm.at[step - 1], r_sc.at[1], to),
        )

    def keep():
        return (
            pltpu.make_async_copy(d.at[pl.ds(4 * x, 4)], quarter(rv0, z, x), local.at[0]),
            pltpu.make_async_copy(meta, m0.at[z], local.at[1]),
        )

    def along_z(piece, way):
        part = quarter(rv0, piece, x)
        to = (r + 1 if way == 0 else r - 1, c)
        return (
            remote(part, part, s_z.at[piece, way], r_z.at[piece], to),
            remote(m0.at[piece], m0.at[piece], s_zm.at[piece, way], r_zm.at[piece], to),
        )

    def chain(piece, way):
        part = quarter(rv1, piece, x, 2 * way, 2)
        send, recv = (s_a, r_a) if way == 0 else (s_b, r_b)
        copies = [remote(part, part, send.at[piece], recv.at[piece], (r + 1 if way == 0 else r - 1, c))]
        if way == 0:
            copies.append(remote(m1.at[piece], m1.at[piece], s_am.at[piece], r_am.at[piece], (r + 1, c)))
        return copies

    def inject(piece, way):
        send, recv = (s_a, r_a) if way == 0 else (s_b, r_b)
        to = (edge, back(2))
        copies = [
            remote(
                quarter(rv0, piece, x, 2 * way, 2),
                quarter(rv1, piece, x, 2 * way, 2),
                send.at[piece],
                recv.at[piece],
                to,
            )
        ]
        if way == 0:
            copies.append(remote(m0.at[piece], m1.at[piece], s_am.at[piece], r_am.at[piece], to))
        return copies

    def ring(way):
        return ((xr if way == 0 else xl) * NZ + z, c)

    def along_x0(piece, way):
        part = quarter(rv0, piece, x)
        return remote(part, part, s_x0.at[piece, way], r_x0.at[piece, way], ring(way))

    def came_x0(piece, way):
        part = quarter(rv0, piece, xl if way == 0 else xr)
        return remote(part, part, s_x0.at[piece, way], r_x0.at[piece, way], ring(way))

    def along_x1(piece, half, way):
        part = quarter(rv1, piece, x, 2 * half, 2)
        return remote(part, part, s_x1.at[piece, half, way], r_x1.at[piece, half, way], ring(way))

    def came_x1(piece, half, way):
        part = quarter(rv1, piece, xl if way == 0 else xr, 2 * half, 2)
        return remote(part, part, s_x1.at[piece, half, way], r_x1.at[piece, half, way], ring(way))

    def onward(buffer, send, recv, piece, way):
        part = quarter(buffer, piece, xl if way == 0 else xr, 2 * way, 2)
        return remote(part, part, send.at[piece, way], recv.at[piece, way], ring(way))

    def came_onward(buffer, send, recv, piece, way):
        part = quarter(buffer, piece, xo, 2 * way, 2)
        return remote(part, part, send.at[piece, way], recv.at[piece, way], ring(way))

    def cross(u):
        part = pl.ds(4 * u, 4)
        return remote(d.at[part], left.at[1, part], s_cr.at[u], r_cr.at[u], (r, back(2)))

    def send_y():
        return remote(d, left.at[3], s_l.at[0], r_l.at[3], (r, back(4)))

    def send_own():
        return remote(d, left.at[0], s_l.at[1], r_l.at[0], (r, sib))

    def pass_cross():
        return remote(left.at[1], left.at[2 * kap], s_l.at[2], r_l.at[2 * kap], (r, sib))

    def pass_cross_y():
        return remote(left.at[1], left.at[4], s_l.at[3], r_l.at[4], (r, back(3)))

    def pass_y():
        return remote(left.at[3], left.at[2 + 2 * kap], s_l.at[4], r_l.at[2 + 2 * kap], (r, sib))

    def came_left(slot):
        return remote(left.at[slot], left.at[slot], s_l.at[0], r_l.at[slot], (r, sib))

    def send_meta(steps):
        return remote(meta, ml.at[steps], s_ml.at[steps - 1], r_ml.at[steps - 1], (r, back(steps)))


    def arrived0(piece):
        along_x0(piece, 0).start()
        along_x0(piece, 1).start()

        @pl.when(jnp.logical_not(up))
        def _():
            for copy in inject(piece, 0):
                copy.start()

        @pl.when(jnp.logical_not(down))
        def _():
            for copy in inject(piece, 1):
                copy.start()

    def z_step(k):
        for way in (0, 1):
            piece = z - k if way == 0 else z + k

            @pl.when(piece >= 0 if way == 0 else piece < NZ)
            def _():
                copies = along_z(piece, way)
                for copy in copies:
                    copy.wait_recv()

                @pl.when(up if way == 0 else down)
                def _():
                    for copy in copies:
                        copy.start()

                arrived0(piece)

    def chain_piece(k, way):
        return 8 - k + z if way == 0 else k - 8 + z

    def chain_step(k):
        for way in (0, 1):
            piece = chain_piece(k, way)

            @pl.when(jnp.logical_and(piece >= 0, piece < NZ))
            def _():
                copies = chain(piece, way)
                for copy in copies:
                    copy.wait_recv()

                @pl.when(up if way == 0 else down)
                def _():
                    for copy in copies:
                        copy.start()

                along_x1(piece, way, 0).start()
                along_x1(piece, way, 1).start()

    def x_piece0(piece):
        for way in (0, 1):
            came_x0(piece, way).wait_recv()
            onward(rv0, s_h0, r_h0, piece, way).start()

    def x_step(k):
        @pl.when(k == 0)
        def _():
            x_piece0(z)

        for way in (0, 1):
            piece = z - k if way == 0 else z + k

            @pl.when(jnp.logical_and(k > 0, piece >= 0 if way == 0 else piece < NZ))
            def _():
                x_piece0(piece)

            behind = chain_piece(k, way)

            @pl.when(jnp.logical_and(behind >= 0, behind < NZ))
            def _():
                came_x1(behind, way, way).wait_recv()
                onward(rv1, s_h1, r_h1, behind, way).start()

    def cross_at(k):
        for u in range(4):
            if isinstance(k, int):
                if CROSS_AT[u] == k:
                    cross(u).start()
            elif CROSS_AT[u] > 0:

                @pl.when(k == CROSS_AT[u])
                def _():
                    cross(u).start()

    @pl.when(source)
    def _():
        for copy in keep():
            copy.start()
        for step in (1, 2, 3):
            for copy in scatter(step):
                copy.start()

    for steps in range(1, 6):
        send_meta(steps).start()
    cross_at(0)
    send_y().start()

    @pl.when(kap == 1)
    def _():
        send_own().start()

    for rv in (rv0, rv1):
        rv[ZERO] = jnp.zeros((BS, BS), jnp.bfloat16)
    own_meta = pltpu.make_async_copy(meta, ml.at[0], local.at[2])
    own_meta.start()

    @pl.when(source)
    def _():
        for copy in keep():
            copy.wait()

    @pl.when(jnp.logical_not(source))
    def _():
        part = quarter(rv0, z, x)
        remote(part, part, s_sc.at[0], r_sc.at[0], (r, sib)).wait_recv()
        remote(m0.at[z], m0.at[z], s_scm.at[0], r_sc.at[1], (r, sib)).wait_recv()

    @pl.when(up)
    def _():
        for copy in along_z(z, 0):
            copy.start()

    @pl.when(down)
    def _():
        for copy in along_z(z, 1):
            copy.start()

    arrived0(z)

    @pl.loop(1, 16 + LAG)
    def _(k):
        z_step(k)
        chain_step(k)
        x_step(k - LAG)
        cross_at(k)

        @pl.when(k == 8)
        def _():
            send_y().wait_recv()
            pass_y().start()

    for u in range(4):
        cross(u).wait_recv()
    pass_cross().start()

    @pl.when(kap == 0)
    def _():
        pass_cross_y().start()

    @pl.loop(0, NZ)
    def _(piece):
        for way in (0, 1):
            came_onward(rv0, s_h0, r_h0, piece, way).wait_recv()

    own_meta.wait()
    for steps in range(1, 6):
        send_meta(steps).wait_recv()
    tables = [
        pltpu.make_async_copy(ml, tl, local.at[3]),
        pltpu.make_async_copy(m0, t0, local.at[4]),
        pltpu.make_async_copy(m1, t1, local.at[5]),
    ]
    for copy in tables:
        copy.start()
    for copy in tables:
        copy.wait()
    came_left(0).wait_recv()
    came_left(2).wait_recv()


    def picks(tile, section, inner, kept):
        group = (2 * c + 4 * tile + 2 * section + (inner >> 3)) % NZ
        table = t1 if tile else t0
        row = 2 * (inner & 7)
        first, second = table[group, 0, row], table[group, 0, row + 1]
        base = group * 16 + row
        return [
            jnp.where(first == wanted, base, jnp.where(second == wanted, base + 1, ZERO)) for wanted in kept
        ]

    def kept_of(section, a):
        return [tl[section, 0, 16 + 4 * a + t] for t in range(4)]

    def terms(total, lefts, rv, spots):
        lhs = jnp.concatenate(lefts, axis=1)
        parts = []
        for pair in (0, 2):
            rhs = jnp.concatenate(
                [jnp.concatenate([rv[spot[pair]], rv[spot[pair + 1]]], axis=1) for spot in spots], axis=0
            )
            parts.append(jnp.dot(lhs, rhs, preferred_element_type=jnp.float32))
        return parts if total is None else [old + new for old, new in zip(total, parts)]

    def send_square(tile, a):
        slot = jnp.where(kap == 0, 3 - 2 * tile, 1 + 2 * tile)
        to = sib if tile == 1 else jnp.where(kap == 0, back(3), sib)
        rows = pl.ds(4 * a, 4)
        return remote(sv.at[2 * tile, rows], sv.at[slot, rows], s_sq.at[tile, a], r_sq.at[slot, a], (r, to))

    def came_square(slot, a):
        rows = pl.ds(4 * a, 4)
        return remote(sv.at[slot, rows], sv.at[slot, rows], s_sq.at[0, a], r_sq.at[slot, a], (r, sib))

    def square(tile, a):
        kept = kept_of(2 * tile, a)
        total = None
        for section in range(4):
            place = 2 * tile + section
            spots = [picks(tile, section, tl[place, 0, 2 * a + i], kept) for i in range(2)]
            lefts = [d[2 * a + i] if place == 0 else left[place - 1, 2 * a + i] for i in range(2)]
            total = terms(total, lefts, rv1 if tile else rv0, spots)
        for t in range(4):
            sv[2 * tile, 4 * a + t] = total[t // 2][:, (t % 2) * BS : (t % 2 + 1) * BS].astype(jnp.bfloat16)
        send_square(tile, a).start()

    def cube(sections, a, total):
        kept = kept_of(0, a)
        for section in sections:
            inner = kept_of(section, a)
            for i in (0, 2):
                spots = [picks(0, section, inner[i + e], kept) for e in range(2)]
                total = terms(total, [sv[section, 4 * a + i + e] for e in range(2)], rv0, spots)
        return total

    @pl.loop(0, 8)
    def _(a):
        square(0, a)

    @pl.loop(0, NZ)
    def _(piece):
        for way in (0, 1):
            came_x1(piece, way, 1 - way).wait_recv()
            came_onward(rv1, s_h1, r_h1, piece, way).wait_recv()

    came_left(4).wait_recv()

    @pl.loop(0, 8)
    def _(a):
        square(1, a)

    @pl.loop(0, 8)
    def _(a):
        total = cube((0, 2), a, None)
        acc[a, 0] = total[0]
        acc[a, 1] = total[1]

    @pl.loop(0, 8)
    def _(a):
        came_square(1, a).wait_recv()
        came_square(3, a).wait_recv()
        total = cube((1, 3), a, [acc[a, 0], acc[a, 1]])
        for t in range(4):
            part = total[t // 2][:, (t % 2) * BS : (t % 2 + 1) * BS]
            out[4 * a + t] = (3.0 * sv[0, 4 * a + t].astype(jnp.float32) - 2.0 * part).astype(jnp.bfloat16)


    @pl.loop(0, NZ)
    def _(piece):
        for way in (0, 1):
            along_x0(piece, way).wait_send()
            onward(rv0, s_h0, r_h0, piece, way).wait_send()
            along_x1(piece, 0, way).wait_send()
            along_x1(piece, 1, way).wait_send()
            onward(rv1, s_h1, r_h1, piece, way).wait_send()
            for copy in chain(piece, way):
                copy.wait_send()

            @pl.when(jnp.logical_and(up, piece <= z) if way == 0 else jnp.logical_and(down, piece >= z))
            def _():
                for copy in along_z(piece, way):
                    copy.wait_send()

        send_square(0, piece).wait_send()
        send_square(1, piece).wait_send()

    for u in range(4):
        cross(u).wait_send()
    for steps in range(1, 6):
        send_meta(steps).wait_send()

    @pl.when(source)
    def _():
        for step in (1, 2, 3):
            for copy in scatter(step):
                copy.wait_send()

    send_y().wait_send()
    pass_cross().wait_send()
    pass_y().wait_send()

    @pl.when(kap == 1)
    def _():
        send_own().wait_send()

    @pl.when(kap == 0)
    def _():
        pass_cross_y().wait_send()


def on_device(density, pattern, kept_pattern):
    own = density.reshape(16, BS, BS)
    meta = jnp.concatenate([pattern.reshape(16), kept_pattern.reshape(32)])
    meta = jnp.pad(meta, (0, 8 * BS - 48)).reshape(8, BS)
    dma = pltpu.SemaphoreType.DMA
    vmem = pl.BlockSpec(memory_space=pltpu.VMEM)
    blocks = lambda *shape: pltpu.VMEM(shape + (BS, BS), jnp.bfloat16)
    table = lambda space, count: space((count, 8, BS), jnp.int32)
    out = pl.pallas_call(
        kernel,
        out_shape=jax.ShapeDtypeStruct((32, BS, BS), jnp.bfloat16),
        in_specs=[vmem, vmem],
        out_specs=vmem,
        scratch_shapes=[
            blocks(5, 16),
            blocks(ZERO + 1),
            blocks(ZERO + 1),
            blocks(4, 32),
            pltpu.VMEM((8, 2, BS, 2 * BS), jnp.float32),
            table(pltpu.VMEM, 6),
            table(pltpu.VMEM, NZ),
            table(pltpu.VMEM, NZ),
            table(pltpu.SMEM, 6),
            table(pltpu.SMEM, NZ),
            table(pltpu.SMEM, NZ),
            dma((3,)),
            dma((3,)),
            dma((2,)),
            dma((6,)),
            dma((NZ, 2)),
            dma((NZ,)),
            dma((NZ, 2)),
            dma((NZ,)),
            dma((NZ,)),
            dma((NZ,)),
            dma((NZ,)),
            dma((NZ,)),
            dma((NZ,)),
            dma((NZ,)),
            dma((NZ, 2)),
            dma((NZ, 2)),
            dma((NZ, 2)),
            dma((NZ, 2)),
            dma((NZ, 2, 2)),
            dma((NZ, 2, 2)),
            dma((NZ, 2)),
            dma((NZ, 2)),
            dma((4,)),
            dma((4,)),
            dma((5,)),
            dma((5,)),
            dma((5,)),
            dma((5,)),
            dma((2, 8)),
            dma((4, 8)),
        ],
        compiler_params=pltpu.CompilerParams(
            collective_id=0, has_side_effects=True, vmem_limit_bytes=40 << 20
        ),
        cost_estimate=pl.CostEstimate(flops=4 << 30, bytes_accessed=12 << 20, transcendentals=0),
        name="purify",
    )(meta, own)
    return out.reshape(8, 1, 4, BS, BS)


def solution(mesh):
    in_specs = (P("row", "col", None, None, None), P("row", "col", None), P("row", "col", None))
    out_specs = P("row", "col", None, None, None)
    return jax.shard_map(
        on_device, mesh=mesh, in_specs=in_specs, out_specs=out_specs, check_vma=False
    )
```

time: 796 us -> 163 us (0.20)
  waiting for transfers between devices: 312 us -> 0 us
  blocking collectives: 206 us -> 0 us
  Pallas kernels: 0 us -> 159 us
  starting transfers between devices: 99.9 us -> 0 us
  local copies, waits for them, and re-layouts: 79.6 us -> 3.62 us
  matrix products: 73.4 us -> 0 us
  between operations: 14 us -> 0.02 us
    psum x1 -> x0, blocking collectives: 206 us -> none  [broadcast(): return lax.psum(jnp.where(mine, array, jnp.zeros_like(array)), axis)]
    psum x1 -> x0, waiting for transfers between devices: 195 us -> none  [broadcast(): return lax.psum(jnp.where(mine, array, jnp.zeros_like(array)), axis)]
    pallas_call x0 -> x1, Pallas kernels: none -> 159 us  [on_device(): pl.pallas_call(kernel, out_shape=jax.ShapeDtypeStruct((32, BS, BS), jnp.b...]
    ppermute x14 -> x0, waiting for transfers between devices: 117 us -> none  [the longest x12 117 us: shifted_2(): return lax.ppermute(value, axis, pairs)]
    ppermute x14 -> x0, starting transfers between devices: 99.8 us -> none  [the longest x12 92.8 us: shifted_2(): return lax.ppermute(value, axis, pairs)]
    dot_general x16 -> x0, matrix products: 73.4 us -> none  [the longest x8 47.2 us: section_terms(): jnp.einsum('aijt,aijxz->atxz', matches, products, precision=lax.Precision...]
    gather x32 -> x0, local copies, waits for them, and re-layouts: 38.6 us -> none  [the longest x16 33 us: section_terms(): picked = jnp.take(right_blocks, left_index, axis=0)]
    transpose x8 -> x0, local copies, waits for them, and re-layouts: 36.1 us -> none  [section_terms(): jnp.einsum('aixy,aijyz->aijxz', left_blocks, picked, preferred_element_ty...]
  transfers between devices with their start and end apart: 15 -> 0, of which waited for: 8 -> 0; matrix products, arithmetic and copies ran while one was open for 15% -> 0% of each run, Pallas kernels for 0% -> 0%
where the time goes in v2:
time: 163 us
  Pallas kernels  159 us (98%)
  local copies, waits for them, and re-layouts  3.62 us (2%)
    pallas_call x1, Pallas kernels, on_device(): pl.pallas_call(kernel, out_shape=jax.ShapeDtypeStruct((32, BS, BS), jnp.b...  159 us
    unnamed x9, local copies, waits for them, and re-layouts  3.46 us

profile of v2, /device:TPU:1, one launch (start us, length us, event | category | flops | bytes accessed | tf_op | source)
XLA Modules:
  0.0 162.6 jit_solution(3953705240660554319)
XLA Ops:
  0.0 0.0 copy-start.2
  0.0 0.7 copy-done.2
  0.7 0.1 copy.7
  0.8 0.0 copy-start.1
  0.8 0.1 reshape.15
  0.8 0.6 copy-done.1
  1.4 0.1 copy.8
  1.5 0.1 reshape.16
  1.6 0.1 pad_add_fusion
  1.7 0.0 copy-start
  1.7 1.0 copy-done
  2.7 158.9 %purify.1 = bf16[32,128,128]{2,1,0:T(8,128)(2,1)S(1)} custom-call(s32[8,128]{1,0:T(8,128)S(1)} %pad_bitcast_fusion.meta, bf16[16,128,128]{2,1,0:T(8,128)(2,1)S(1)} %bitcast.11), custom_call_target="tpu_custom_call" | custom-call | flops 4294967296 | bytes 12582912 | tf_op jit(solution)/shard_map/purify/pallas_call | solution.py:484
  161.6 1.0 copy.11
  (1 shorter events, 0.0 us)
Async XLA Ops:
  0.0 0.7 copy-start.2
  0.8 0.7 copy-start.1
  1.7 1.0 copy-start

commit v3 on v2

v3 whole, which is shorter than its diff:
```python
import jax
import jax.numpy as jnp
from jax import lax
from jax.experimental import pallas as pl
from jax.experimental.pallas import tpu as pltpu
from jax.sharding import PartitionSpec as P

MESH = pl.DeviceIdType.MESH
ROWS, COLS = 32, 16
NX, NZ = 4, 8
BS = 128
ZERO = 128
LAG = 2
BEHIND = 1
STEPS = 7 + BEHIND + LAG
CROSS_AT = (0, 6, 8, 10)


def remote(src, dst, send, recv, device):
    return pltpu.make_async_remote_copy(
        src_ref=src, dst_ref=dst, send_sem=send, recv_sem=recv, device_id=device, device_id_type=MESH
    )


def kernel(
    meta, held, out,
    d, left, rv0, rv1, sv, acc, ml, m0, m1, tl, t0, t1,
    s_sc, s_scm, r_sc, local,
    s_z, r_z, s_zm, r_zm,
    s_i, s_im, s_c, r_c, s_cm, r_cm,
    s_x0, r_x0, s_h0, r_h0, s_x1, r_x1, s_h1, r_h1,
    s_cr, r_cr, s_pc, r_pc, s_py, r_py, s_l, r_l, s_ml, r_ml, s_sq, r_sq,
):
    r, c = lax.axis_index("row"), lax.axis_index("col")
    x, z, kap = r // NZ, r % NZ, c % 2
    sib = c + 1 - 2 * kap
    xr, xl, xo = (x + 1) % NX, (x + 3) % NX, (x + 2) % NX
    up, down = z < NZ - 1, z > 0
    deep = z % 4
    source = (r - 2 * c + ROWS) % ROWS < NZ
    top, bottom = jnp.logical_not(up), jnp.logical_not(down)
    middle = jnp.logical_or(z == 3, z == 4)
    bands = (
        (rv0, m0, s_x0, r_x0, s_h0, r_h0),
        (rv1, m1, s_x1, r_x1, s_h1, r_h1),
    )

    def back(steps):
        return (c + COLS - steps) % COLS

    def ahead(steps):
        return (c + steps) % COLS

    own = pltpu.make_async_copy(held, d, local.at[6])
    own.start()
    for rv in (rv0, rv1):
        rv[ZERO] = jnp.zeros((BS, BS), jnp.bfloat16)
    barrier = pltpu.get_barrier_semaphore()

    def greet(device):
        pl.semaphore_signal(barrier, inc=1, device_id=device, device_id_type=MESH)

    for steps in range(1, 6):
        greet((r, back(steps)))
        greet((r, ahead(steps)))
    for other in (xr, xl, xo):
        greet((other * NZ + z, c))

    @pl.when(up)
    def _():
        greet((r + 1, c))

    @pl.when(down)
    def _():
        greet((r - 1, c))

    @pl.when(top)
    def _():
        greet((r - 7, back(2)))
        greet((r - 3, back(2)))
        greet((r - 7, ahead(2)))

    @pl.when(bottom)
    def _():
        greet((r + 7, back(2)))
        greet((r + 3, back(2)))
        greet((r + 7, ahead(2)))

    @pl.when(z == 4)
    def _():
        greet((r + 3, ahead(2)))

    @pl.when(z == 3)
    def _():
        greet((r - 3, ahead(2)))

    ends = jnp.logical_or(top, bottom)
    pl.semaphore_wait(barrier, jnp.where(ends, 17, jnp.where(middle, 16, 15)))
    own.wait()


    def quarter(buffer, piece, which, start=0, size=4):
        return buffer.at[pl.ds(piece * 16 + 4 * which + start, size)]

    def scatter(step):
        other = (x + step) % NX
        to = (other * NZ + z, c)
        return (
            remote(d.at[pl.ds(4 * other, 4)], quarter(rv0, z, other), s_sc.at[step - 1], r_sc.at[0], to),
            remote(meta, m0.at[z], s_scm.at[step - 1], r_sc.at[1], to),
        )

    def keep():
        return (
            pltpu.make_async_copy(d.at[pl.ds(4 * x, 4)], quarter(rv0, z, x), local.at[0]),
            pltpu.make_async_copy(meta, m0.at[z], local.at[1]),
        )

    def along_z(piece, half, way):
        part = quarter(rv0, piece, x, 2 * half, 2)
        to = (r + 1 if way == 0 else r - 1, c)
        copies = [remote(part, part, s_z.at[piece, half, way], r_z.at[piece, half], to)]
        if half == 0:
            copies.append(remote(m0.at[piece], m0.at[piece], s_zm.at[piece, way], r_zm.at[piece], to))
        return copies

    def chain(piece, half, way):
        part = quarter(rv1, piece, x, 2 * half, 2)
        to = (r + 1 if way == 0 else r - 1, c)
        copies = [remote(part, part, s_c.at[piece, half], r_c.at[piece, half], to)]
        if half == 0:
            copies.append(remote(m1.at[piece], m1.at[piece], s_cm.at[piece], r_cm.at[piece], to))
        return copies

    def inject(piece, half, way):
        copies = []
        for entry in (0, 1):
            distance = (7, 3)[entry]
            to = (r - distance if way == 0 else r + distance, back(2))
            copies.append(
                remote(
                    quarter(rv0, piece, x, 2 * half, 2),
                    quarter(rv1, piece, x, 2 * half, 2),
                    s_i.at[piece, half, entry],
                    r_c.at[piece, half],
                    to,
                )
            )
            if half == 0:
                copies.append(remote(m0.at[piece], m1.at[piece], s_im.at[piece, entry], r_cm.at[piece], to))
        return copies

    def ring(way):
        return ((xr if way == 0 else xl) * NZ + z, c)

    def along_x(tile, piece, half, way):
        rv, _, send, recv, _, _ = bands[tile]
        part = quarter(rv, piece, x, 2 * half, 2)
        return remote(part, part, send.at[piece, half, way], recv.at[piece, half, way], ring(way))

    def came_x(tile, piece, half, way):
        rv, _, send, recv, _, _ = bands[tile]
        part = quarter(rv, piece, xl if way == 0 else xr, 2 * half, 2)
        return remote(part, part, send.at[piece, half, way], recv.at[piece, half, way], ring(way))

    def onward(tile, piece, way):
        rv, _, _, _, send, recv = bands[tile]
        part = quarter(rv, piece, xl if way == 0 else xr, 2 * way, 2)
        return remote(part, part, send.at[piece, way], recv.at[piece, way], ring(way))

    def came_onward(tile, piece, way):
        rv, _, _, _, send, recv = bands[tile]
        part = quarter(rv, piece, xo, 2 * way, 2)
        return remote(part, part, send.at[piece, way], recv.at[piece, way], ring(way))

    def cross(u):
        part = pl.ds(4 * u, 4)
        return remote(d.at[part], left.at[1, part], s_cr.at[u], r_cr.at[u], (r, back(2)))

    def pass_cross(u):
        part = pl.ds(4 * u, 4)
        return remote(left.at[1, part], left.at[2 * kap, part], s_pc.at[u], r_pc.at[u], (r, sib))

    def came_pass(u):
        part = left.at[2 - 2 * kap, pl.ds(4 * u, 4)]
        return remote(part, part, s_pc.at[u], r_pc.at[u], (r, sib))

    def pass_cross_y(u):
        part = pl.ds(4 * u, 4)
        return remote(left.at[1, part], left.at[4, part], s_py.at[u], r_py.at[u], (r, back(3)))

    def send_y():
        return remote(d, left.at[3], s_l.at[0], r_l.at[0], (r, back(4)))

    def send_own():
        return remote(d, left.at[0], s_l.at[1], r_l.at[1], (r, sib))

    def pass_y():
        return remote(left.at[3], left.at[2 + 2 * kap], s_l.at[2], r_l.at[2], (r, sib))

    def came_y():
        part = left.at[4 - 2 * kap]
        return remote(part, part, s_l.at[2], r_l.at[2], (r, sib))

    def send_meta(steps):
        return remote(meta, ml.at[steps], s_ml.at[steps - 1], r_ml.at[steps - 1], (r, back(steps)))


    def arrived0(piece, half):
        along_x(0, piece, half, 0).start()
        along_x(0, piece, half, 1).start()

        @pl.when(jnp.logical_and(top, piece >= 4))
        def _():
            for copy in inject(piece, half, 0):
                copy.start()

        @pl.when(jnp.logical_and(bottom, piece < 4))
        def _():
            for copy in inject(piece, half, 1):
                copy.start()

    def z_step(k):
        for way in (0, 1):
            piece = z - k if way == 0 else z + k

            @pl.when(piece >= 0 if way == 0 else piece < NZ)
            def _():
                for half in (0, 1):
                    copies = along_z(piece, half, way)
                    for copy in copies:
                        copy.wait_recv()

                    @pl.when(up if way == 0 else down)
                    def _():
                        for copy in copies:
                            copy.start()

                    arrived0(piece, half)

    def chain_order(k, way):
        return k - 1 - BEHIND - (deep if way == 0 else 3 - deep)

    def chain_on(way):
        return deep < 3 if way == 0 else deep > 0

    def chain_step(k):
        for way in (0, 1):
            order = chain_order(k, way)
            piece = 7 - order if way == 0 else order

            @pl.when(jnp.logical_and(order >= 0, order < 4))
            def _():
                for half in (0, 1):
                    copies = chain(piece, half, way)
                    for copy in copies:
                        copy.wait_recv()

                    @pl.when(chain_on(way))
                    def _():
                        for copy in copies:
                            copy.start()

                    along_x(1, piece, half, 0).start()
                    along_x(1, piece, half, 1).start()

    def x_piece(tile, piece):
        for way in (0, 1):
            came_x(tile, piece, way, way).wait_recv()
            onward(tile, piece, way).start()

    def x_step(k):
        @pl.when(k == 0)
        def _():
            x_piece(0, z)

        for way in (0, 1):
            piece = z - k if way == 0 else z + k

            @pl.when(jnp.logical_and(k > 0, piece >= 0 if way == 0 else piece < NZ))
            def _():
                x_piece(0, piece)

        for way in (0, 1):
            order = chain_order(k, way)

            @pl.when(jnp.logical_and(order >= 0, order < 4))
            def _():
                x_piece(1, 7 - order if way == 0 else order)

    @pl.when(source)
    def _():
        for copy in keep():
            copy.start()
        for step in (1, 2, 3):
            for copy in scatter(step):
                copy.start()

    for steps in range(1, 6):
        send_meta(steps).start()
    for u in range(4):
        if CROSS_AT[u] == 0:
            cross(u).start()
    send_y().start()

    @pl.when(kap == 1)
    def _():
        send_own().start()

    own_meta = pltpu.make_async_copy(meta, ml.at[0], local.at[2])
    own_meta.start()

    @pl.when(source)
    def _():
        for copy in keep():
            copy.wait()

    @pl.when(jnp.logical_not(source))
    def _():
        part = quarter(rv0, z, x)
        remote(part, part, s_sc.at[0], r_sc.at[0], (r, sib)).wait_recv()
        remote(m0.at[z], m0.at[z], s_scm.at[0], r_sc.at[1], (r, sib)).wait_recv()

    for half in (0, 1):

        @pl.when(up)
        def _():
            for copy in along_z(z, half, 0):
                copy.start()

        @pl.when(down)
        def _():
            for copy in along_z(z, half, 1):
                copy.start()

        arrived0(z, half)

    @pl.loop(1, STEPS + 1)
    def _(k):
        z_step(k)
        chain_step(k)
        x_step(k - LAG)
        for u in range(4):
            if CROSS_AT[u] > 0:

                @pl.when(k == CROSS_AT[u])
                def _():
                    cross(u).start()

        @pl.when(k == 6)
        def _():
            send_y().wait_recv()
            pass_y().start()

    own_meta.wait()
    for steps in range(1, 6):
        send_meta(steps).wait_recv()
    tables = [
        pltpu.make_async_copy(ml, tl, local.at[3]),
        pltpu.make_async_copy(m0, t0, local.at[4]),
        pltpu.make_async_copy(m1, t1, local.at[5]),
    ]
    for copy in tables:
        copy.start()

    @pl.loop(0, NZ)
    def _(piece):
        for way in (0, 1):
            came_x(0, piece, way, 1 - way).wait_recv()
            came_onward(0, piece, way).wait_recv()

    for copy in tables:
        copy.wait()

    @pl.when(kap == 0)
    def _():
        send_own().wait_recv()

    came_y().wait_recv()


    def picks(tile, section, inner, kept):
        group = (2 * c + 4 * tile + 2 * section + (inner >> 3)) % NZ
        table = t1 if tile else t0
        row = 2 * (inner & 7)
        first, second = table[group, 0, row], table[group, 0, row + 1]
        base = group * 16 + row
        return [
            jnp.where(first == wanted, base, jnp.where(second == wanted, base + 1, ZERO)) for wanted in kept
        ]

    def kept_of(section, a):
        return [tl[section, 0, 16 + 4 * a + t] for t in range(4)]

    def terms(total, lefts, rv, spots):
        lhs = jnp.concatenate(lefts, axis=1)
        parts = []
        for pair in (0, 2):
            rhs = jnp.concatenate(
                [jnp.concatenate([rv[spot[pair]], rv[spot[pair + 1]]], axis=1) for spot in spots], axis=0
            )
            parts.append(jnp.dot(lhs, rhs, preferred_element_type=jnp.float32))
        return parts if total is None else [old + new for old, new in zip(total, parts)]

    def send_square(tile, a):
        slot = jnp.where(kap == 0, 3 - 2 * tile, 1 + 2 * tile)
        to = sib if tile == 1 else jnp.where(kap == 0, back(3), sib)
        rows = pl.ds(4 * a, 4)
        return remote(sv.at[2 * tile, rows], sv.at[slot, rows], s_sq.at[tile, a], r_sq.at[slot, a], (r, to))

    def came_square(slot, a):
        rows = pl.ds(4 * a, 4)
        return remote(sv.at[slot, rows], sv.at[slot, rows], s_sq.at[0, a], r_sq.at[slot, a], (r, sib))

    def square(tile, a):
        kept = kept_of(2 * tile, a)
        total = None
        for section in range(4):
            place = 2 * tile + section
            spots = [picks(tile, section, tl[place, 0, 2 * a + i], kept) for i in range(2)]
            lefts = [d[2 * a + i] if place == 0 else left[place - 1, 2 * a + i] for i in range(2)]
            total = terms(total, lefts, rv1 if tile else rv0, spots)
        for t in range(4):
            sv[2 * tile, 4 * a + t] = total[t // 2][:, (t % 2) * BS : (t % 2 + 1) * BS].astype(jnp.bfloat16)
        send_square(tile, a).start()

    def cube(sections, a, total):
        kept = kept_of(0, a)
        for section in sections:
            inner = kept_of(section, a)
            for i in (0, 2):
                spots = [picks(0, section, inner[i + e], kept) for e in range(2)]
                total = terms(total, [sv[section, 4 * a + i + e] for e in range(2)], rv0, spots)
        return total

    def keep_total(a, total):
        acc[a, 0] = total[0]
        acc[a, 1] = total[1]

    @pl.loop(0, 4)
    def _(u):
        cross(u).wait_recv()
        pass_cross(u).start()

        @pl.when(kap == 0)
        def _():
            pass_cross_y(u).start()

        came_pass(u).wait_recv()
        for a in (2 * u, 2 * u + 1):
            square(0, a)
        for a in (2 * u, 2 * u + 1):
            keep_total(a, cube((0,), a, None))

    @pl.loop(0, NZ)
    def _(piece):
        for way in (0, 1):
            came_x(1, piece, way, 1 - way).wait_recv()
            came_onward(1, piece, way).wait_recv()

    @pl.loop(0, 4)
    def _(u):
        @pl.when(kap == 1)
        def _():
            pass_cross_y(u).wait_recv()

        for a in (2 * u, 2 * u + 1):
            square(1, a)

    @pl.loop(0, 8)
    def _(a):
        keep_total(a, cube((2,), a, [acc[a, 0], acc[a, 1]]))


    @pl.loop(0, NZ)
    def _(piece):
        for way in (0, 1):
            for tile in (0, 1):
                along_x(tile, piece, 0, way).wait_send()
                along_x(tile, piece, 1, way).wait_send()
                onward(tile, piece, way).wait_send()

            @pl.when(jnp.logical_and(up, piece <= z) if way == 0 else jnp.logical_and(down, piece >= z))
            def _():
                for half in (0, 1):
                    for copy in along_z(piece, half, way):
                        copy.wait_send()

            mine = piece >= 4 if way == 0 else piece < 4

            @pl.when(jnp.logical_and(chain_on(way), mine))
            def _():
                for half in (0, 1):
                    for copy in chain(piece, half, way):
                        copy.wait_send()

            @pl.when(jnp.logical_and(top if way == 0 else bottom, mine))
            def _():
                for half in (0, 1):
                    for copy in inject(piece, half, way):
                        copy.wait_send()

    for u in range(4):
        cross(u).wait_send()
        pass_cross(u).wait_send()
    for steps in range(1, 6):
        send_meta(steps).wait_send()

    @pl.when(source)
    def _():
        for step in (1, 2, 3):
            for copy in scatter(step):
                copy.wait_send()

    send_y().wait_send()
    pass_y().wait_send()

    @pl.when(kap == 1)
    def _():
        send_own().wait_send()

    @pl.when(kap == 0)
    def _():
        for u in range(4):
            pass_cross_y(u).wait_send()

    @pl.loop(0, 8)
    def _(a):
        came_square(1, a).wait_recv()
        came_square(3, a).wait_recv()
        total = cube((1, 3), a, [acc[a, 0], acc[a, 1]])
        for t in range(4):
            part = total[t // 2][:, (t % 2) * BS : (t % 2 + 1) * BS]
            out[4 * a + t] = (3.0 * sv[0, 4 * a + t].astype(jnp.float32) - 2.0 * part).astype(jnp.bfloat16)
        send_square(0, a).wait_send()
        send_square(1, a).wait_send()


def on_device(density, pattern, kept_pattern):
    own = density.reshape(16, BS, BS)
    meta = jnp.concatenate([pattern.reshape(16), kept_pattern.reshape(32)])
    meta = jnp.pad(meta, (0, 8 * BS - 48)).reshape(8, BS)
    dma = pltpu.SemaphoreType.DMA
    vmem = pl.BlockSpec(memory_space=pltpu.VMEM)
    blocks = lambda *shape: pltpu.VMEM(shape + (BS, BS), jnp.bfloat16)
    table = lambda space, count: space((count, 8, BS), jnp.int32)
    out = pl.pallas_call(
        kernel,
        out_shape=jax.ShapeDtypeStruct((32, BS, BS), jnp.bfloat16),
        in_specs=[vmem, pl.BlockSpec(memory_space=pl.ANY)],
        out_specs=vmem,
        scratch_shapes=[
            blocks(16),
            blocks(5, 16),
            blocks(ZERO + 1),
            blocks(ZERO + 1),
            blocks(4, 32),
            pltpu.VMEM((8, 2, BS, 2 * BS), jnp.float32),
            table(pltpu.VMEM, 6),
            table(pltpu.VMEM, NZ),
            table(pltpu.VMEM, NZ),
            table(pltpu.SMEM, 6),
            table(pltpu.SMEM, NZ),
            table(pltpu.SMEM, NZ),
            dma((3,)),
            dma((3,)),
            dma((2,)),
            dma((7,)),
            dma((NZ, 2, 2)),
            dma((NZ, 2)),
            dma((NZ, 2)),
            dma((NZ,)),
            dma((NZ, 2, 2)),
            dma((NZ, 2)),
            dma((NZ, 2)),
            dma((NZ, 2)),
            dma((NZ,)),
            dma((NZ,)),
            dma((NZ, 2, 2)),
            dma((NZ, 2, 2)),
            dma((NZ, 2)),
            dma((NZ, 2)),
            dma((NZ, 2, 2)),
            dma((NZ, 2, 2)),
            dma((NZ, 2)),
            dma((NZ, 2)),
            dma((4,)),
            dma((4,)),
            dma((4,)),
            dma((4,)),
            dma((4,)),
            dma((4,)),
            dma((3,)),
            dma((3,)),
            dma((5,)),
            dma((5,)),
            dma((2, 8)),
            dma((4, 8)),
        ],
        compiler_params=pltpu.CompilerParams(
            collective_id=0, has_side_effects=True, vmem_limit_bytes=40 << 20
        ),
        cost_estimate=pl.CostEstimate(flops=4 << 30, bytes_accessed=12 << 20, transcendentals=0),
        name="purify",
    )(meta, own)
    return out.reshape(8, 1, 4, BS, BS)


def solution(mesh):
    in_specs = (P("row", "col", None, None, None), P("row", "col", None), P("row", "col", None))
    out_specs = P("row", "col", None, None, None)
    return jax.shard_map(
        on_device, mesh=mesh, in_specs=in_specs, out_specs=out_specs, check_vma=False
    )
```

time: 163 us -> 133 us (0.82)
  Pallas kernels: 159 us -> 129 us
    pallas_call x1, Pallas kernels: 159 us -> 129 us  [on_device(): pl.pallas_call(kernel, out_shape=jax.ShapeDtypeStruct((32, BS, BS), jnp.b...]
where the time goes in v3:
time: 133 us; the launch traced here: 132 us
  Pallas kernels  129 us (97%)
  local copies, waits for them, and re-layouts  3.62 us (3%)
    pallas_call x1, Pallas kernels, on_device(): pl.pallas_call(kernel, out_shape=jax.ShapeDtypeStruct((32, BS, BS), jnp.b...  129 us
    unnamed x9, local copies, waits for them, and re-layouts  3.46 us

profile of v3, /device:TPU:1, one launch (start us, length us, event | category | flops | bytes accessed | tf_op | source)
XLA Modules:
  0.0 132.5 jit_solution(2359766670689095528)
XLA Ops:
  0.0 0.0 copy-start.2
  0.0 0.7 copy-done.2
  0.7 0.1 copy.7
  0.8 0.0 copy-start.1
  0.8 0.1 reshape.15
  0.8 0.6 copy-done.1
  1.4 0.1 copy.8
  1.5 0.1 reshape.16
  1.6 0.1 pad_add_fusion
  1.7 0.0 copy-start
  1.7 1.0 copy-done
  2.7 128.7 %purify.1 = bf16[32,128,128]{2,1,0:T(8,128)(2,1)S(1)} custom-call(s32[8,128]{1,0:T(8,128)S(1)} %pad_bitcast_fusion.meta, bf16[16,128,128]{2,1,0:T(8,128)(2,1)S(1)} %bitcast.11), custom_call_target="tpu_custom_call" | custom-call | flops 4294967296 | bytes 12582912 | tf_op jit(solution)/shard_map/purify/pallas_call | solution.py:547
  131.5 1.0 copy.11
  (1 shorter events, 0.0 us)
Async XLA Ops:
  0.0 0.7 copy-start.2
  0.8 0.7 copy-start.1
  1.7 1.0 copy-start

commit v4 on v3

--- a/solution.py
+++ b/solution.py
@@ -23,8 +23,8 @@
 
 
 def kernel(
-    meta, held, out,
-    d, left, rv0, rv1, sv, acc, ml, m0, m1, tl, t0, t1,
+    pattern, kept_pattern, held, out,
+    meta, d, left, rv0, rv1, sv, acc, ml, m0, m1, tl, t0, t1,
     s_sc, s_scm, r_sc, local,
     s_z, r_z, s_zm, r_zm,
     s_i, s_im, s_c, r_c, s_cm, r_cm,
@@ -53,6 +53,9 @@
 
     own = pltpu.make_async_copy(held, d, local.at[6])
     own.start()
+    meta[...] = jnp.zeros_like(meta)
+    meta[0:2, 0:8] = pattern[...]
+    meta[2:6, 0:8] = kept_pattern[...]
     for rv in (rv0, rv1):
         rv[ZERO] = jnp.zeros((BS, BS), jnp.bfloat16)
     barrier = pltpu.get_barrier_semaphore()
@@ -383,14 +386,14 @@
         group = (2 * c + 4 * tile + 2 * section + (inner >> 3)) % NZ
         table = t1 if tile else t0
         row = 2 * (inner & 7)
-        first, second = table[group, 0, row], table[group, 0, row + 1]
+        first, second = table[group, 0, inner & 7], table[group, 1, inner & 7]
         base = group * 16 + row
         return [
             jnp.where(first == wanted, base, jnp.where(second == wanted, base + 1, ZERO)) for wanted in kept
         ]
 
     def kept_of(section, a):
-        return [tl[section, 0, 16 + 4 * a + t] for t in range(4)]
+        return [tl[section, 2 + t, a] for t in range(4)]
 
     def terms(total, lefts, rv, spots):
         lhs = jnp.concatenate(lefts, axis=1)
@@ -417,7 +420,7 @@
         total = None
         for section in range(4):
             place = 2 * tile + section
-            spots = [picks(tile, section, tl[place, 0, 2 * a + i], kept) for i in range(2)]
+            spots = [picks(tile, section, tl[place, i, a], kept) for i in range(2)]
             lefts = [d[2 * a + i] if place == 0 else left[place - 1, 2 * a + i] for i in range(2)]
             total = terms(total, lefts, rv1 if tile else rv0, spots)
         for t in range(4):
@@ -538,8 +541,6 @@
 
 def on_device(density, pattern, kept_pattern):
     own = density.reshape(16, BS, BS)
-    meta = jnp.concatenate([pattern.reshape(16), kept_pattern.reshape(32)])
-    meta = jnp.pad(meta, (0, 8 * BS - 48)).reshape(8, BS)
     dma = pltpu.SemaphoreType.DMA
     vmem = pl.BlockSpec(memory_space=pltpu.VMEM)
     blocks = lambda *shape: pltpu.VMEM(shape + (BS, BS), jnp.bfloat16)
@@ -547,9 +548,10 @@
     out = pl.pallas_call(
         kernel,
         out_shape=jax.ShapeDtypeStruct((32, BS, BS), jnp.bfloat16),
-        in_specs=[vmem, pl.BlockSpec(memory_space=pl.ANY)],
+        in_specs=[vmem, vmem, pl.BlockSpec(memory_space=pltpu.HBM)],
         out_specs=vmem,
         scratch_shapes=[
+            pltpu.VMEM((8, BS), jnp.int32),
             blocks(16),
             blocks(5, 16),
             blocks(ZERO + 1),
@@ -602,7 +604,7 @@
         ),
         cost_estimate=pl.CostEstimate(flops=4 << 30, bytes_accessed=12 << 20, transcendentals=0),
         name="purify",
-    )(meta, own)
+    )(pattern[:, 0].T, kept_pattern[:, 0].T, own)
     return out.reshape(8, 1, 4, BS, BS)
 
 

time: 133 us -> 132 us (level)
    unnamed x9 -> x7, local copies, waits for them, and re-layouts: 3.46 us -> 2.71 us
where the time goes in v4:
time: 132 us; the launch traced here: 131 us
  Pallas kernels  129 us (98%)
  local copies, waits for them, and re-layouts  2.71 us (2%)
    pallas_call x1, Pallas kernels, on_device(): pl.pallas_call(kernel, out_shape=jax.ShapeDtypeStruct((32, BS, BS), jnp.b...  129 us
    unnamed x7, local copies, waits for them, and re-layouts  2.71 us

profile of v4, /device:TPU:1, one launch (start us, length us, event | category | flops | bytes accessed | tf_op | source)
XLA Modules:
  0.0 131.4 jit_solution(16036605105617847242)
XLA Ops:
  0.0 0.0 copy-start.1
  0.0 0.0 copy-start.2
  0.0 0.7 copy-done.1
  0.7 0.0 copy-done.2
  0.7 0.0 copy-start
  0.7 1.0 copy-done
  1.7 128.7 %purify.1 = bf16[32,128,128]{2,1,0:T(8,128)(2,1)S(1)} custom-call(s32[2,8]{1,0:T(2,128)S(1)} %bitcast.13, s32[4,8]{1,0:T(4,128)S(1)} %bitcast.12, bf16[16,128,128]{2,1,0:T(8,128)(2,1)S(1)} %bitcast.11), custom_call_target="tpu_custom_call" | custom-call | flops 4294967296 | bytes 12582912 | tf_op jit(solution)/shard_map/purify/pallas_call | solution.py:548
  130.5 1.0 copy.6
Async XLA Ops:
  0.0 0.7 copy-start.1
  0.0 0.7 copy-start.2
  0.7 1.0 copy-start
